TPU v7x, 256 devices: a whole 4x4x8 slice. The times are simulated.
256 devices in a mesh: row: 16 (over y, z_lo, core), col: 16 (over x, z_hi).
Axes of the slice: x: 4, y: 4, z: 8 (z_hi: 4, z_lo: 2; z = z_hi * 2 + z_lo), core: 2. Of those that a mesh axis runs over, the one named last changes fastest.
Arguments:
- left_states: int32 [512, 8192], P(None, 'row'), may hold values from 0 to 3
- right_states: int32 [512, 4096], P(None, 'col'), may hold values from 0 to 3
- left_bias: float32 [4, 8192], P(None, 'row'), may hold values from -5 to 5
- right_bias: float32 [4, 4096], P(None, 'col'), may hold values from -5 to 5
- couplings: bfloat16 [4, 8192, 4, 4096], P(None, 'row', None, 'col'), may hold values from -0.09375 to 0.09375
Outputs:
- left_residual: bfloat16 [512, 4, 8192], P(None, None, 'row')
- right_residual: bfloat16 [512, 4, 4096], P(None, None, 'col')
- coupling_grad: bfloat16 [4, 8192, 4, 4096], P(None, 'row', None, 'col')
All inputs are finite; a program needn't handle non-finite values.
Results may differ from a plain program's by a relative error of at most 0.011.
Values may be sent and summed in bfloat16 or wider, within the bound.
A program may use at most 128 MiB of HBM per device.

v0:
```python
import jax
import jax.numpy as jnp
from jax import lax
from jax.sharding import PartitionSpec as P


def residual_of(fields, bias, onehot):
    shaped = fields.reshape(onehot.shape) + bias[None]
    exps = jnp.exp(shaped)
    probs = exps / jnp.sum(exps, axis=1, keepdims=True)
    return (onehot.astype(jnp.float32) - probs).astype(jnp.bfloat16)


def body(left_states, right_states, left_bias, right_bias, couplings):
    genomes = left_states.shape[0]
    states = couplings.shape[0]
    left_width = couplings.shape[1]
    right_width = couplings.shape[3]
    state_ids = jnp.arange(states, dtype=jnp.int32)
    left_onehot = (left_states[:, None, :] == state_ids[None, :, None]).astype(jnp.bfloat16)
    right_onehot = (right_states[:, None, :] == state_ids[None, :, None]).astype(jnp.bfloat16)
    left_flat = left_onehot.reshape(genomes, states * left_width)
    right_flat = right_onehot.reshape(genomes, states * right_width)
    matrix = couplings.reshape(states * left_width, states * right_width)
    piece = right_flat
    left_summed = lax.psum(
        lax.dot_general(
            piece, matrix, (((1,), (1,)), ((), ())), preferred_element_type=jnp.float32
        ).astype(jnp.bfloat16),
        "col",
    ).astype(jnp.float32)
    left_residual = residual_of(left_summed, left_bias, left_onehot)
    piece = left_flat
    right_summed = lax.psum(jnp.dot(piece, matrix, preferred_element_type=jnp.float32), "row")
    right_residual = residual_of(right_summed, right_bias, right_onehot)
    stacked_left = jnp.concatenate(
        [left_residual.reshape(genomes, states * left_width), left_flat], axis=0
    )
    stacked_right = jnp.concatenate(
        [right_flat, right_residual.reshape(genomes, states * right_width)], axis=0
    )
    summed = lax.dot_general(
        stacked_left, stacked_right, (((0,), (0,)), ((), ())), preferred_element_type=jnp.float32
    )
    coupling_grad = (-summed).astype(jnp.bfloat16).reshape(states, left_width, states, right_width)
    return (left_residual, right_residual, coupling_grad)


def solution(mesh):
    in_specs = (
        P(None, "row"),
        P(None, "col"),
        P(None, "row"),
        P(None, "col"),
        P(None, "row", None, "col"),
    )
    out_specs = (P(None, None, "row"), P(None, None, "col"), P(None, "row", None, "col"))
    return jax.shard_map(body, mesh=mesh, in_specs=in_specs, out_specs=out_specs, check_vma=False)
```

profile of v0, /device:TPU:16, one launch (start us, length us, event | category | flops | bytes accessed | tf_op | source)
XLA Modules:
  0.0 379.5 jit_solution(3303184345068325128)
XLA Ops:
  7.2 0.0 all-reduce.5.cloned.1.call-start
  7.2 0.0 copy-start.9
  7.2 2.3 iota_compare_fusion
  9.6 0.6 copy.10
  10.2 0.0 copy-done.9
  10.2 3.1 copy.9
  13.3 0.0 copy-start.7
  13.3 5.9 %fusion.11 = f32[512,1024]{1,0:T(8,128)} fusion(pred[512,2048]{1,0:T(8,128)(4,1)S(1)} %bitcast.40, bf16[2048,1024]{1,0:T(8,128)(2,1)} %bitcast.4), kind=kOutput, calls=%fused_computation.25 | convolution fusion | flops 2147483648 | bytes 7340032 | tf_op jit(solution)/shard_map/dot_general | solution.py:34
  19.2 0.0 all-reduce.5.cloned.1.call-update
  19.2 0.0 all-reduce.3.cloned.1.call-start
  19.3 0.0 copy-done.7
  19.3 0.6 iota_compare_fusion.1
  19.9 0.3 copy.8
  20.1 0.0 copy-start.11
  20.2 0.0 copy-start.10
  20.2 5.9 %convolution_convert_fusion = bf16[512,2048]{1,0:T(8,128)(2,1)} fusion(pred[512,1024]{1,0:T(8,128)(4,1)S(1)} %bitcast.41, bf16[2048,1024]{1,0:T(8,128)(2,1)} %bitcast.4), kind=kOutput, calls=%fused_computation.11 | convolution fusion | flops 2148532224 | bytes 6815744 | tf_op jit(solution)/shard_map/dot_general | solution.py:27
  26.1 0.0 copy-start.2
  26.1 0.0 all-reduce.3.cloned.1.call-update
  26.1 0.0 copy-done.11
  26.1 0.0 copy-done.10
  26.2 0.4 eq.73
  26.5 1.8 copy.15
  28.3 0.0 copy-done.2
  28.3 0.7 eq.70
  29.1 3.9 %copy.11 = s32[64,8,4,512]{3,1,2,0:T(8,128)} copy(s32[64,8,4,512]{3,2,1,0:T(4,128)S(1)} %bitcast.30) | data formatting | bytes 8388608
  32.9 110.0 %all-reduce.5.cloned.1.call-done = f32[512,1024]{1,0:T(8,128)} async-done(((f32[512,1024]{1,0:T(8,128)}), f32[512,1024]{1,0:T(8,128)}) %all-reduce.5.cloned.1.call-update) | async-done | bytes 2097168 | tf_op jit(solution)/shard_map/psum | solution.py:34
  142.9 2.2 reshape.106
  145.1 0.0 copy-start.8
  145.1 1.5 fusion.9
  146.7 0.4 div.28
  147.1 1.8 copy.18
  148.9 0.0 copy-done.8
  148.9 2.1 fusion.8
  151.0 184.5 %all-reduce.3.cloned.1.call-done = bf16[512,2048]{1,0:T(8,128)(2,1)} async-done(((bf16[512,2048]{1,0:T(8,128)(2,1)}), bf16[512,2048]{1,0:T(8,128)(2,1)}) %all-reduce.3.cloned.1.call-update) | async-done | bytes 2097168 | tf_op jit(solution)/shard_map/psum | solution.py:26
  335.5 6.0 %reshape.105 = f32[512,4,512]{2,1,0:T(4,128)} reshape(bf16[512,2048]{1,0:T(8,128)(2,1)} %all-reduce.3.cloned.1.call-done) | data formatting | bytes 6291456 | tf_op jit(solution)/shard_map/reshape | solution.py:8
  341.5 0.0 copy-start
  341.5 5.5 %fusion.4 = f32[512,512]{1,0:T(8,128)S(1)} fusion(f32[512,4,512]{2,1,0:T(4,128)} %reshape.105, f32[4,512]{1,0:T(4,128)S(1)} %copy-done.10), kind=kLoop, calls=%fused_computation.10 | loop fusion | flops 1835008 | bytes 5251072 | tf_op jit(solution)/shard_map/reduce_sum | solution.py:10
  347.0 0.0 copy-done
  347.0 3.5 fusion.3
  350.5 0.7 div.26
  351.2 0.0 copy-start.3
  351.3 0.0 copy-start.4
  351.3 0.0 copy-start.5
  351.3 2.0 copy.14
  353.3 0.0 copy-done.3
  353.3 0.1 copy-done.4
  353.5 0.6 copy-done.5
  354.1 0.0 copy-start.1
  354.1 0.0 copy-start.6
  354.1 0.9 subtract_convert_fusion.1
  355.0 1.3 copy-done.1
  356.3 0.7 copy-done.6
  357.0 1.6 subtract_convert_fusion
  358.6 6.2 %negate_convert_fusion = bf16[2048,1024]{1,0:T(8,128)(2,1)} fusion(bf16[512,2048]{1,0:T(8,128)(2,1)S(1)} %get-tuple-element.6, bf16[512,2048]{1,0:T(8,128)(2,1)S(1)} %get-tuple-element.5, bf16[512,1024]{1,0:T(8,128)(2,1)S(1)} %get-tuple-element.3, bf16[512,1024]{1,0:T(8,128)(2,1)S(1)} %get-tuple-element.4), kind=kOutput, calls=%fused_computation | convolution fusion | flops 4311744512 | bytes 10485760 | tf_op jit(solution)/shard_map/dot_general | solution.py:42
  364.8 7.8 %reshape.107 = bf16[4,512,4,256]{3,2,1,0:T(4,128)(2,1)} reshape(bf16[2048,1024]{1,0:T(8,128)(2,1)} %negate_convert_fusion) | data formatting | bytes 8388608 | tf_op jit(solution)/shard_map/reshape | solution.py:45
  (6 shorter events, 0.0 us)
Async XLA Ops:
  7.2 135.7 %all-reduce.5.cloned.1.call-start = ((), (), s32[]{:S(2)}) async-start(), calls=%async_computation.1 | async-start | bytes 4194304 | tf_op jit(solution)/shard_map/psum | solution.py:34
  7.2 3.0 copy-start.9
  13.3 6.0 %copy-start.7 = (s32[512,256]{1,0:T(8,128)S(1)}, s32[512,256]{1,0:T(8,128)}, u32[]{:S(2)}) copy-start(s32[512,256]{1,0:T(8,128)} %param.6) | copy-start | bytes 1572868
  19.2 316.3 %all-reduce.3.cloned.1.call-start = ((), (), s32[]{:S(2)}) async-start(), calls=%async_computation | async-start | bytes 4194304 | tf_op jit(solution)/shard_map/psum | solution.py:26
  20.1 5.9 %copy-start.11 = (f32[4,256]{1,0:T(4,128)S(1)}, f32[4,256]{1,0:T(4,128)}, u32[]{:S(2)}) copy-start(f32[4,256]{1,0:T(4,128)} %param.8) | copy-start | bytes 12292
  20.2 6.0 %copy-start.10 = (f32[4,512]{1,0:T(4,128)S(1)}, f32[4,512]{1,0:T(4,128)}, u32[]{:S(2)}) copy-start(f32[4,512]{1,0:T(4,128)} %param.7) | copy-start | bytes 24580
  26.1 2.3 copy-start.2
  145.1 3.8 copy-start.8
  341.5 5.5 %copy-start = (f32[512,4,512]{2,1,0:T(4,128)S(1)}, f32[512,4,512]{2,1,0:T(4,128)}, u32[]{:S(2)}) copy-start(f32[512,4,512]{2,1,0:T(4,128)} %reshape.105) | copy-start | bytes 12582916
  351.2 2.1 copy-start.3
  351.3 2.2 copy-start.4
  351.3 2.8 copy-start.5
  354.1 2.2 copy-start.1
  354.1 2.9 copy-start.6
Sparse Core Ops, SparseCore 0:
  19.3 123.5 all-reduce.4
  146.1 189.3 all-reduce.2
where the time goes:
time: 380 us; the launch traced here: 379 us
  waiting for transfers between devices  295 us (78%)
  local copies, waits for them, and re-layouts  34.5 us (9%)
  other arithmetic  18.1 us (5%)
  matrix products  18.1 us (5%)
  between operations  14.3 us (4%)
    psum x1, waiting for transfers between devices, body(): lax.psum(lax.dot_general(piece, matrix, (((1,), (1,)), ((), ())), preferr...  185 us
    psum x1, waiting for transfers between devices, body(): lax.psum(jnp.dot(piece, matrix, preferred_element_type=jnp.float32), 'row')  110 us
    unnamed x37, local copies, waits for them, and re-layouts  16.3 us
    reshape x2, local copies, waits for them, and re-layouts, residual_of(): shaped = fields.reshape(onehot.shape) + bias[None]  8.2 us
    convert_element_type x4, other arithmetic, residual_of(): return (onehot.astype(jnp.float32) - probs).astype(jnp.bfloat16)  8.06 us
    reshape x1, local copies, waits for them, and re-layouts, body(): (-summed).astype(jnp.bfloat16)  7.83 us
  transfers between devices with their start and end apart: 2, of which 2 were waited for; matrix products, arithmetic and copies ran while one was open for 6% of the time, Pallas kernels for 0%

commit v1 on v0

v1 whole, which is shorter than its diff:
```python
import jax
import jax.numpy as jnp
from jax import lax
from jax.experimental import pallas as pl
from jax.experimental.pallas import tpu as pltpu
from jax.sharding import PartitionSpec as P

MESH = pl.DeviceIdType.MESH
BF = jnp.bfloat16
F32 = jnp.float32
PIECES = 4
VMEM_LIMIT = 56 * 1024 * 1024


def permutation(rows, inner):
    outer = rows // inner
    at = lax.broadcasted_iota(jnp.int32, (rows, rows), 0)
    of = lax.broadcasted_iota(jnp.int32, (rows, rows), 1)
    want = lax.rem(at, outer) * inner + lax.div(at, outer)
    return jnp.where(of == want, 1.0, 0.0).astype(BF)


def onehot(states, value):
    return jnp.where(states == value, 1.0, 0.0).astype(BF)


def softmax_residual(diffs, states):
    top = jnp.maximum(jnp.maximum(diffs[0], diffs[1]), jnp.maximum(diffs[2], 0.0))
    exps = [jnp.exp(d - top) for d in diffs]
    inverse = 1.0 / (exps[0] + exps[1] + exps[2] + jnp.exp(-top))
    return [
        (jnp.where(states == a, 1.0, 0.0) - exps[a] * inverse).astype(BF) for a in range(3)
    ]


def exchange_kernel(
    left_ref, right_ref, lbias_ref, rbias_ref, coup_ref,
    rg_out, rr_out,
    raw, flat, perm, rt, loh, slt, bt,
    lp, xa, xb, zp, za, zb, rg,
    cs, cr, own, yp, ya, yb, tz, zs, zr, rr,
    in_sem, out_sem, lsend, lrecv, rsend, rrecv,
):
    row = lax.axis_index("row")
    col = lax.axis_index("col")
    core = lax.rem(row, 2)
    zl = lax.rem(lax.div(row, 2), 2)
    y = lax.div(row, 4)
    x = lax.div(col, 4)
    z = lax.rem(col, 4)

    def at_x(v):
        return {"row": row, "col": lax.rem(v, 4) * 4 + z}

    def at_z(v):
        return {"row": row, "col": x * 4 + lax.rem(v, 4)}

    def at_y(v):
        return {"row": lax.rem(v, 4) * 4 + zl * 2 + core, "col": col}

    x_next, x_prev, z_next, z_prev = at_x(x + 1), at_x(x + 3), at_z(z + 1), at_z(z + 3)
    y_next, y_prev = at_y(y + 1), at_y(y + 3)
    core_peer = {"row": y * 4 + zl * 2 + 1 - core, "col": col}
    zl_peer = {"row": y * 4 + (1 - zl) * 2 + core, "col": col}
    peers = (x_next, x_prev, z_next, z_prev, y_next, y_prev, core_peer, zl_peer)

    barrier = pltpu.get_barrier_semaphore()
    for peer in peers:
        pl.semaphore_signal(barrier, inc=1, device_id=peer, device_id_type=MESH)

    loads = []
    for p in range(PIECES):
        rows = pl.ds(p * 1024, 1024)
        load = pltpu.make_async_copy(coup_ref.at[:, rows, :], raw.at[:, rows, :], in_sem.at[p])
        load.start()
        loads.append(load)

    sent = []

    def send(src, dst, sems, slot, peer):
        copy = pltpu.make_async_remote_copy(
            src_ref=src, dst_ref=dst, send_sem=sems[0].at[slot], recv_sem=sems[1].at[slot],
            device_id=peer, device_id_type=MESH,
        )
        copy.start()
        sent.append(copy)
        return copy

    lsems = (lsend, lrecv)
    rsems = (rsend, rrecv)

    perm[...] = permutation(256, 8)
    right_t = right_ref[...].T
    for b in range(4):
        rt[pl.ds(b * 256, 256), :] = onehot(right_t, b)

    live = {}

    def s0(p):
        loads[p].wait()
        for a in range(4):
            for h in range(2):
                pair = [
                    raw[a, pl.ds(p * 1024 + (2 * h + k) * 256, 256), :] for k in range(2)
                ]
                turned = jnp.dot(
                    perm[...], jnp.concatenate(pair, axis=1), preferred_element_type=F32
                ).astype(BF)
                for k in range(2):
                    for jt in range(2):
                        for b in range(4):
                            flat[
                                pl.ds(a * 512 + p * 128 + (2 * h + k) * 32, 32),
                                pl.ds(b * 256 + jt * 128, 128),
                            ] = turned[(jt * 4 + b) * 32:(jt * 4 + b + 1) * 32, k * 128:(k + 1) * 128]
        lhs = jnp.concatenate([flat[pl.ds(a * 512 + p * 128, 128), :] for a in range(4)], axis=0)
        fields = jnp.dot(lhs, rt[...], preferred_element_type=F32)
        for a in range(3):
            diff = (fields[a * 128:(a + 1) * 128] - fields[384:512]).astype(BF)
            for xc in range(4):
                for zc in range(4):
                    lp[p, xc, zc, a] = diff[zc * 32:(zc + 1) * 32, xc * 128:(xc + 1) * 128]

    def s0_send(p):
        opp, nxt, prv = lax.rem(x + 2, 4), lax.rem(x + 1, 4), lax.rem(x + 3, 4)
        lo, hi = pl.ds(0, 2), pl.ds(2, 2)
        live[p, 0] = send(lp.at[p, opp, lo], xa.at[p, 0], lsems, p * 20 + 0, x_next)
        live[p, 1] = send(lp.at[p, opp, hi], xa.at[p, 1], lsems, p * 20 + 1, x_prev)
        live[p, 2] = send(lp.at[p, nxt, hi], xb.at[p, 0, hi], lsems, p * 20 + 2, x_next)
        live[p, 3] = send(lp.at[p, prv, lo], xb.at[p, 1, lo], lsems, p * 20 + 3, x_prev)

    def s1(p):
        nxt, prv = lax.rem(x + 1, 4), lax.rem(x + 3, 4)
        lo, hi = pl.ds(0, 2), pl.ds(2, 2)
        live[p, 0].wait_recv()
        lp[p, nxt, lo] = (lp[p, nxt, lo].astype(F32) + xa[p, 0].astype(F32)).astype(BF)
        live[p, 4] = send(lp.at[p, nxt, lo], xb.at[p, 0, lo], lsems, p * 20 + 4, x_next)
        live[p, 1].wait_recv()
        lp[p, prv, hi] = (lp[p, prv, hi].astype(F32) + xa[p, 1].astype(F32)).astype(BF)
        live[p, 5] = send(lp.at[p, prv, hi], xb.at[p, 1, hi], lsems, p * 20 + 5, x_prev)

    def s2(p):
        for m in (2, 3, 4, 5):
            live[p, m].wait_recv()
        zp[p] = (
            lp[p, x].astype(F32) + xb[p, 0].astype(F32) + xb[p, 1].astype(F32)
        ).astype(BF)
        opp, nxt, prv = lax.rem(z + 2, 4), lax.rem(z + 1, 4), lax.rem(z + 3, 4)
        lo, hi = pl.ds(0, 16), pl.ds(16, 16)
        live[p, 6] = send(zp.at[p, opp, :, lo], za.at[p, 0], lsems, p * 20 + 6, z_next)
        live[p, 7] = send(zp.at[p, opp, :, hi], za.at[p, 1], lsems, p * 20 + 7, z_prev)
        live[p, 8] = send(zp.at[p, nxt, :, hi], zb.at[p, 0, :, hi], lsems, p * 20 + 8, z_next)
        live[p, 9] = send(zp.at[p, prv, :, lo], zb.at[p, 1, :, lo], lsems, p * 20 + 9, z_prev)

    def s3(p):
        nxt, prv = lax.rem(z + 1, 4), lax.rem(z + 3, 4)
        lo, hi = pl.ds(0, 16), pl.ds(16, 16)
        live[p, 6].wait_recv()
        zp[p, nxt, :, lo] = (zp[p, nxt, :, lo].astype(F32) + za[p, 0].astype(F32)).astype(BF)
        live[p, 10] = send(zp.at[p, nxt, :, lo], zb.at[p, 0, :, lo], lsems, p * 20 + 10, z_next)
        live[p, 7].wait_recv()
        zp[p, prv, :, hi] = (zp[p, prv, :, hi].astype(F32) + za[p, 1].astype(F32)).astype(BF)
        live[p, 11] = send(zp.at[p, prv, :, hi], zb.at[p, 1, :, hi], lsems, p * 20 + 11, z_prev)

    def s4(p):
        for m in (8, 9, 10, 11):
            live[p, m].wait_recv()
        total = zp[p, z].astype(F32) + zb[p, 0].astype(F32) + zb[p, 1].astype(F32)
        rows = pl.ds(pl.multiple_of(p * 128 + z * 32, 32), 32)
        diffs = [total[a] + bt[a, rows, :] for a in range(3)]
        result = softmax_residual(diffs, slt[x, rows, :])
        for a in range(3):
            rg[p, x, z, a] = result[a]
        block = rg.at[p, x, z]
        live[p, 12] = send(block, block, lsems, p * 20 + 12, z_next)
        live[p, 13] = send(block, block, lsems, p * 20 + 13, z_prev)

    def s5(p):
        nxt, prv = lax.rem(z + 1, 4), lax.rem(z + 3, 4)
        live[p, 12].wait_recv()
        block = rg.at[p, x, prv, :, pl.ds(0, 16)]
        live[p, 14] = send(block, block, lsems, p * 20 + 14, z_next)
        live[p, 13].wait_recv()
        block = rg.at[p, x, nxt, :, pl.ds(16, 16)]
        live[p, 15] = send(block, block, lsems, p * 20 + 15, z_prev)

    def s6(p):
        live[p, 14].wait_recv()
        live[p, 15].wait_recv()
        block = rg.at[p, x]
        live[p, 16] = send(block, block, lsems, p * 20 + 16, x_next)
        live[p, 17] = send(block, block, lsems, p * 20 + 17, x_prev)

    def s7(p):
        nxt, prv = lax.rem(x + 1, 4), lax.rem(x + 3, 4)
        live[p, 16].wait_recv()
        block = rg.at[p, prv, pl.ds(0, 2)]
        live[p, 18] = send(block, block, lsems, p * 20 + 18, x_next)
        live[p, 17].wait_recv()
        block = rg.at[p, nxt, pl.ds(2, 2)]
        live[p, 19] = send(block, block, lsems, p * 20 + 19, x_prev)

    finals = []

    def s8(p):
        live[p, 18].wait_recv()
        live[p, 19].wait_recv()
        copy = pltpu.make_async_copy(rg.at[p], rg_out.at[p], out_sem.at[p])
        copy.start()
        finals.append(copy)

    def right_diffs(half):
        lhs = loh[pl.ds(pl.multiple_of(half * 256, 256), 256), :]
        fields = jnp.dot(lhs, flat[...], preferred_element_type=F32)
        return [fields[:, b * 256:(b + 1) * 256] - fields[:, 768:1024] for b in range(3)]

    def r0():
        for b, diff in enumerate(right_diffs(1 - core)):
            cs[:, pl.ds(b * 256, 256)] = diff.astype(BF)
        live["c"] = send(cs, cr, rsems, 0, core_peer)
        for b, diff in enumerate(right_diffs(core)):
            own[:, pl.ds(b * 256, 256)] = diff

    def r1():
        live["c"].wait_recv()
        for c in range(4):
            rows = pl.ds(c * 64, 64)
            yp[c] = (own[rows, :] + cr[rows, :].astype(F32)).astype(BF)
        opp, nxt, prv = lax.rem(y + 2, 4), lax.rem(y + 1, 4), lax.rem(y + 3, 4)
        lo, hi = pl.ds(0, 32), pl.ds(32, 32)
        live["y0"] = send(yp.at[opp, lo], ya.at[0], rsems, 1, y_next)
        live["y1"] = send(yp.at[opp, hi], ya.at[1], rsems, 2, y_prev)
        live["y2"] = send(yp.at[nxt, hi], yb.at[0, hi], rsems, 3, y_next)
        live["y3"] = send(yp.at[prv, lo], yb.at[1, lo], rsems, 4, y_prev)

    def r2():
        nxt, prv = lax.rem(y + 1, 4), lax.rem(y + 3, 4)
        lo, hi = pl.ds(0, 32), pl.ds(32, 32)
        live["y0"].wait_recv()
        yp[nxt, lo] = (yp[nxt, lo].astype(F32) + ya[0].astype(F32)).astype(BF)
        live["y4"] = send(yp.at[nxt, lo], yb.at[0, lo], rsems, 5, y_next)
        live["y1"].wait_recv()
        yp[prv, hi] = (yp[prv, hi].astype(F32) + ya[1].astype(F32)).astype(BF)
        live["y5"] = send(yp.at[prv, hi], yb.at[1, hi], rsems, 6, y_prev)

    def r3():
        for name in ("y2", "y3", "y4", "y5"):
            live[name].wait_recv()
        total = yp[y].astype(F32) + yb[0].astype(F32) + yb[1].astype(F32)
        tz[0] = total[:32]
        tz[1] = total[32:]
        zs[...] = tz[1 - zl].astype(BF)
        live["z0"] = send(zs, zr, rsems, 7, zl_peer)

    def rows_at(core_at, y_at, zl_at, count):
        return pl.ds(pl.multiple_of(core_at * 256 + y_at * 64 + zl_at * 32, 32), count)

    def r4():
        live["z0"].wait_recv()
        total = tz[zl] + zr[...].astype(F32)
        rows = rows_at(core, y, zl, 32)
        base = rbias_ref[pl.ds(3, 1), :]
        diffs = [
            total[:, b * 256:(b + 1) * 256] + (rbias_ref[pl.ds(b, 1), :] - base) for b in range(3)
        ]
        for b, part in enumerate(softmax_residual(diffs, right_ref[rows, :])):
            rr[rows, pl.ds(b * 256, 256)] = part
        block = rr.at[rows, :]
        live["z1"] = send(block, block, rsems, 8, zl_peer)

    def r5():
        live["z1"].wait_recv()
        block = rr.at[rows_at(core, y, 0, 64), :]
        live["y6"] = send(block, block, rsems, 9, y_next)
        live["y7"] = send(block, block, rsems, 10, y_prev)

    def r6():
        nxt, prv = lax.rem(y + 1, 4), lax.rem(y + 3, 4)
        live["y6"].wait_recv()
        block = rr.at[rows_at(core, prv, 0, 32), :]
        live["y8"] = send(block, block, rsems, 11, y_next)
        live["y7"].wait_recv()
        block = rr.at[rows_at(core, nxt, 1, 32), :]
        live["y9"] = send(block, block, rsems, 12, y_prev)

    def r7():
        live["y8"].wait_recv()
        live["y9"].wait_recv()
        block = rr.at[rows_at(core, 0, 0, 256), :]
        live["c1"] = send(block, block, rsems, 13, core_peer)

    def r8():
        live["c1"].wait_recv()
        copy = pltpu.make_async_copy(rr, rr_out, out_sem.at[PIECES])
        copy.start()
        finals.append(copy)

    def left_tables():
        left_t = left_ref[...].T
        for xc in range(4):
            slt[xc] = left_t[:, xc * 128:(xc + 1) * 128]
        base = lbias_ref[pl.ds(3, 1), :]
        for a in range(3):
            diff = lbias_ref[pl.ds(a, 1), :] - base
            for p in range(PIECES):
                part = jnp.broadcast_to(diff[:, p * 128:(p + 1) * 128], (128, 128))
                bt[a, pl.ds(p * 128, 128), :] = part.T

    def left_onehots():
        states = left_ref[...]
        for a in range(4):
            loh[:, pl.ds(a * 512, 512)] = onehot(states, a)

    s0(0)
    pl.semaphore_wait(barrier, len(peers))
    s0_send(0)
    left_stages = (None, s1, s2, s3, s4, s5, s6, s7, s8)
    right_stages = (r0, r1, r2, r3, r4, r5, r6, r7, r8)
    for tick in range(1, PIECES + 9):
        if tick < PIECES:
            s0(tick)
            s0_send(tick)
        if tick == 1:
            left_tables()
        if tick == 2:
            left_onehots()
        for p in range(PIECES):
            if 0 < tick - p < 9:
                left_stages[tick - p](p)
        if 0 <= tick - PIECES + 1 < 9:
            right_stages[tick - PIECES + 1]()
    for copy in sent:
        copy.wait_send()
    for copy in finals:
        copy.wait()


def exchange(left_states, right_states, left_bias, right_bias, couplings):
    vmem = pl.BlockSpec(memory_space=pltpu.VMEM)
    hbm = pl.BlockSpec(memory_space=pl.ANY)
    n = PIECES
    return pl.pallas_call(
        exchange_kernel,
        out_shape=(
            jax.ShapeDtypeStruct((n, 4, 4, 3, 32, 128), BF),
            jax.ShapeDtypeStruct((512, 768), BF),
        ),
        in_specs=[vmem] * 4 + [hbm],
        out_specs=(hbm, hbm),
        scratch_shapes=[
            pltpu.VMEM((4, 4096, 128), BF),
            pltpu.VMEM((2048, 1024), BF),
            pltpu.VMEM((256, 256), BF),
            pltpu.VMEM((1024, 512), BF),
            pltpu.VMEM((512, 2048), BF),
            pltpu.VMEM((4, 512, 128), jnp.int32),
            pltpu.VMEM((3, 512, 128), F32),
            pltpu.VMEM((n, 4, 4, 3, 32, 128), BF),
            pltpu.VMEM((n, 2, 2, 3, 32, 128), BF),
            pltpu.VMEM((n, 2, 4, 3, 32, 128), BF),
            pltpu.VMEM((n, 4, 3, 32, 128), BF),
            pltpu.VMEM((n, 2, 3, 16, 128), BF),
            pltpu.VMEM((n, 2, 3, 32, 128), BF),
            pltpu.VMEM((n, 4, 4, 3, 32, 128), BF),
            pltpu.VMEM((256, 768), BF),
            pltpu.VMEM((256, 768), BF),
            pltpu.VMEM((256, 768), F32),
            pltpu.VMEM((4, 64, 768), BF),
            pltpu.VMEM((2, 32, 768), BF),
            pltpu.VMEM((2, 64, 768), BF),
            pltpu.VMEM((2, 32, 768), F32),
            pltpu.VMEM((32, 768), BF),
            pltpu.VMEM((32, 768), BF),
            pltpu.VMEM((512, 768), BF),
            pltpu.SemaphoreType.DMA((n,)),
            pltpu.SemaphoreType.DMA((n + 1,)),
            pltpu.SemaphoreType.DMA((n * 20,)),
            pltpu.SemaphoreType.DMA((n * 20,)),
            pltpu.SemaphoreType.DMA((14,)),
            pltpu.SemaphoreType.DMA((14,)),
        ],
        compiler_params=pltpu.CompilerParams(
            collective_id=0, has_side_effects=True, vmem_limit_bytes=VMEM_LIMIT
        ),
        name="exchange",
    )(left_states, right_states, left_bias, right_bias, couplings)


def gradient_kernel(left_ref, right_ref, rg_ref, rr_ref, lres_ref, rres_ref, grad_ref, rhs, perm, perm16):
    g = pl.program_id(0)

    @pl.when(g == 0)
    def _():
        perm[...] = permutation(256, 32)
        perm16[...] = permutation(256, 16)
        states = right_ref[...]
        total = jnp.zeros((512, 256), F32)
        for b in range(4):
            rhs[pl.ds(0, 512), pl.ds(b * 256, 256)] = -onehot(states, b)
        for b in range(3):
            part = rr_ref[:, pl.ds(b * 256, 256)]
            rhs[pl.ds(512, 512), pl.ds(b * 256, 256)] = -part
            total += part.astype(F32)
        rhs[pl.ds(512, 512), pl.ds(768, 256)] = total.astype(BF)

    rows = pl.ds(pl.multiple_of(512 + g * 128, 128), 128)
    part = -rhs[rows, :]
    for h in range(2):
        stack = jnp.concatenate(
            [
                jnp.concatenate(
                    [
                        part[(2 * h + k) * 32:(2 * h + k + 1) * 32, b * 256 + jt * 128:b * 256 + (jt + 1) * 128]
                        for jt in range(2) for b in range(4)
                    ],
                    axis=0,
                )
                for k in range(2)
            ],
            axis=1,
        )
        turned = jnp.dot(perm[...], stack, preferred_element_type=F32).astype(BF)
        for k in range(2):
            rres_ref[pl.ds((2 * h + k) * 256, 256), :] = turned[:, k * 128:(k + 1) * 128]

    natural = []
    for p in range(PIECES):
        blocks = [rg_ref[p, g, :, a].reshape(128, 128).astype(F32) for a in range(3)]
        blocks.append(-(blocks[0] + blocks[1] + blocks[2]))
        natural.extend([block.T.astype(BF) for block in blocks])
    for h in range(4):
        stack = jnp.concatenate(
            [
                jnp.concatenate([block[(2 * h + k) * 16:(2 * h + k + 1) * 16] for block in natural], axis=0)
                for k in range(2)
            ],
            axis=1,
        )
        turned = jnp.dot(perm16[...], stack, preferred_element_type=F32).astype(BF)
        for k in range(2):
            lres_ref[pl.ds((2 * h + k) * 256, 256), :] = turned[:, k * 128:(k + 1) * 128]

    left_t = left_ref[...].T
    parts = [
        jnp.concatenate([rg_ref[g, xc, :, a].reshape(128, 128) for xc in range(4)], axis=1)
        for a in range(3)
    ]
    last = -(parts[0].astype(F32) + parts[1].astype(F32) + parts[2].astype(F32))
    parts.append(last.astype(BF))
    lhs = jnp.concatenate(
        [jnp.concatenate([parts[a], onehot(left_t, a)], axis=1) for a in range(4)], axis=0
    )
    summed = jnp.dot(lhs, rhs[...], preferred_element_type=F32).astype(BF)
    for a in range(4):
        for h in range(2):
            stack = jnp.concatenate(
                [
                    jnp.concatenate(
                        [
                            summed[
                                a * 128 + (2 * h + k) * 32:a * 128 + (2 * h + k + 1) * 32,
                                b * 256 + jt * 128:b * 256 + (jt + 1) * 128,
                            ]
                            for jt in range(2) for b in range(4)
                        ],
                        axis=0,
                    )
                    for k in range(2)
                ],
                axis=1,
            )
            turned = jnp.dot(perm[...], stack, preferred_element_type=F32).astype(BF)
            for k in range(2):
                grad_ref[a, pl.ds((2 * h + k) * 256, 256), :] = turned[:, k * 128:(k + 1) * 128]


def gradient(left_states, right_states, rg, rr):
    whole = pl.BlockSpec(memory_space=pltpu.VMEM)
    return pl.pallas_call(
        gradient_kernel,
        grid=(PIECES,),
        out_shape=(
            jax.ShapeDtypeStruct((8192, 128), BF),
            jax.ShapeDtypeStruct((4096, 128), BF),
            jax.ShapeDtypeStruct((4, 4096, 128), BF),
        ),
        in_specs=[pl.BlockSpec((512, 128), lambda g: (0, g)), whole, whole, whole],
        out_specs=(
            pl.BlockSpec((2048, 128), lambda g: (g, 0)),
            pl.BlockSpec((1024, 128), lambda g: (g, 0)),
            pl.BlockSpec((4, 1024, 128), lambda g: (0, g, 0)),
        ),
        scratch_shapes=[
            pltpu.VMEM((1024, 1024), BF),
            pltpu.VMEM((256, 256), BF),
            pltpu.VMEM((256, 256), BF),
        ],
        compiler_params=pltpu.CompilerParams(vmem_limit_bytes=VMEM_LIMIT),
        name="gradient",
    )(left_states, right_states, rg, rr)


def body(left_states, right_states, left_bias, right_bias, couplings):
    view = couplings.reshape(4, 512, 4, 2, 128).transpose(0, 1, 3, 2, 4).reshape(4, 4096, 128)
    rg, rr = exchange(left_states, right_states, left_bias, right_bias, view)
    left, right, grad = gradient(left_states, right_states, rg, rr)
    left_residual = left.reshape(512, 4, 4, 128).transpose(0, 2, 1, 3).reshape(512, 4, 512)
    right_residual = right.reshape(512, 2, 4, 128).transpose(0, 2, 1, 3).reshape(512, 4, 256)
    coupling_grad = grad.reshape(4, 512, 2, 4, 128).transpose(0, 1, 3, 2, 4).reshape(4, 512, 4, 256)
    return left_residual, right_residual, coupling_grad


def solution(mesh):
    in_specs = (
        P(None, "row"),
        P(None, "col"),
        P(None, "row"),
        P(None, "col"),
        P(None, "row", None, "col"),
    )
    out_specs = (P(None, None, "row"), P(None, None, "col"), P(None, "row", None, "col"))
    return jax.shard_map(body, mesh=mesh, in_specs=in_specs, out_specs=out_specs, check_vma=False)
```

time: 380 us -> 70.4 us (0.19)
  waiting for transfers between devices: 295 us -> 0 us
  Pallas kernels: 0 us -> 69.1 us
  local copies, waits for them, and re-layouts: 34.5 us -> 0 us
  matrix products: 18.1 us -> 0 us
  other arithmetic: 18.1 us -> 0 us
  between operations: 14.3 us -> 0.64 us
    psum x2 -> x0, waiting for transfers between devices: 294 us -> none  [the longest x1 185 us: body(): lax.psum(lax.dot_general(piece, matrix, (((1,), (1,)), ((), ())), preferr...]
    pallas_call x0 -> x2, Pallas kernels: none -> 69.1 us  [the longest x1 58 us: exchange(): pl.pallas_call(exchange_kernel, out_shape=(jax.ShapeDtypeStruct((n, 4, 4,...]
    dot_general x3 -> x0, matrix products: 18.1 us -> none  [the longest x1 6.22 us: body(): lax.dot_general(stacked_left, stacked_right, (((0,), (0,)), ((), ())), pr...]
    unnamed x37 -> x0, local copies, waits for them, and re-layouts: 16.3 us -> none
    reshape x3 -> x0, local copies, waits for them, and re-layouts: 16 us -> none  [the longest x2 8.2 us: residual_of(): shaped = fields.reshape(onehot.shape) + bias[None]]
    convert_element_type x4 -> x0, other arithmetic: 8.06 us -> none  [residual_of(): return (onehot.astype(jnp.float32) - probs).astype(jnp.bfloat16)]
    reduce_sum x2 -> x0, other arithmetic: 7.07 us -> none  [residual_of(): probs = exps / jnp.sum(exps, axis=1, keepdims=True)]
  transfers between devices with their start and end apart: 2 -> 0, of which waited for: 2 -> 0; matrix products, arithmetic and copies ran while one was open for 6% -> 0% of each run, Pallas kernels for 0% -> 0%
where the time goes in v1:
time: 70.4 us; the launch traced here: 69.7 us
  Pallas kernels  69.1 us (98%)
    pallas_call x1, Pallas kernels, exchange(): pl.pallas_call(exchange_kernel, out_shape=(jax.ShapeDtypeStruct((n, 4, 4,...  58 us
    pallas_call x1, Pallas kernels, gradient(): pl.pallas_call(gradient_kernel, grid=(PIECES,), out_shape=(jax.ShapeDtype...  11.1 us

profile of v1, /device:TPU:16, one launch (start us, length us, event | category | flops | bytes accessed | tf_op | source)
XLA Modules:
  0.0 69.7 jit_solution(9362120027788275175)
XLA Ops:
  0.6 58.0 %exchange.1 = (bf16[4,4,4,3,32,128]{5,4,3,2,1,0:T(8,128)(2,1)}, bf16[512,768]{1,0:T(8,128)(2,1)}) custom-call(s32[512,512]{1,0:T(8,128)} %left_ref.3, s32[512,256]{1,0:T(8,128)} %right_ref.3, f32[4,512]{1,0:T(4,128)} %lbias_ref.1, f32[4,256]{1,0:T(4,128)} %rbias_ref.1, bf16[4,4096,128]{2,1,0:T(8,128)(2,1)} %bitcast.20), custom_call_target="tpu_custom_call" | custom-call | tf_op jit(solution)/shard_map/exchange/pallas_call | solution.py:342
  58.6 11.1 %gradient.1 = (bf16[8192,128]{1,0:T(8,128)(2,1)}, bf16[4096,128]{1,0:T(8,128)(2,1)}, bf16[4,4096,128]{2,1,0:T(8,128)(2,1)}) custom-call(s32[512,512]{1,0:T(8,128)} %left_ref.3, s32[512,256]{1,0:T(8,128)} %right_ref.3, bf16[4,4,4,3,32,128]{5,4,3,2,1,0:T(8,128)(2,1)} %get-tuple-element.8.rg_ref, bf16[512,768]{1,0:T(8,128)(2,1)} %get-tuple-element.9.rr_ref), custom_call_target="tpu_custom_call" | custom-call | tf_op jit(solution)/shard_map/gradient/pallas_call | solution.py:479

commit v2 on v0

v2 whole, which is shorter than its diff:
```python
import jax
import jax.numpy as jnp
from jax import lax
from jax.experimental import pallas as pl
from jax.experimental.pallas import tpu as pltpu
from jax.sharding import PartitionSpec as P

MESH = pl.DeviceIdType.MESH
BF = jnp.bfloat16
F32 = jnp.float32
PIECES = 4
DIRECT_SCATTER = (0,)
DIRECT_GATHER = (3,)
EXCHANGE_VMEM = 40 * 1024 * 1024
FINISH_VMEM = 24 * 1024 * 1024


def permutation(inner_bits):
    outer_bits = 8 - inner_bits
    at = lax.broadcasted_iota(jnp.int32, (256, 256), 0)
    of = lax.broadcasted_iota(jnp.int32, (256, 256), 1)
    want = ((at & ((1 << outer_bits) - 1)) << inner_bits) + (at >> outer_bits)
    return jnp.where(of == want, 1.0, 0.0).astype(BF)


def side_by_side(blocks):
    return jnp.concatenate([jnp.concatenate(rows, axis=0) for rows in blocks], axis=1)


def spread_states(perm, values, store):
    for h in range(values.shape[0] // 64):
        stack = side_by_side(
            [
                [
                    values[(2 * h + k) * 32:(2 * h + k + 1) * 32, b * 256 + jt * 128:b * 256 + (jt + 1) * 128]
                    for jt in range(2) for b in range(4)
                ]
                for k in range(2)
            ]
        )
        turned = jnp.dot(perm, stack, preferred_element_type=F32).astype(BF)
        for k in range(2):
            store(2 * h + k, turned[:, k * 128:(k + 1) * 128])


def four_states(parts):
    last = -(parts[0].astype(F32) + parts[1].astype(F32) + parts[2].astype(F32))
    return list(parts) + [last.astype(BF)]


def piece_rows(rg):
    return four_states(
        [
            jnp.concatenate([rg[xc, :, a].reshape(128, 128) for xc in range(4)], axis=1)
            for a in range(3)
        ]
    )


def onehot(states, value):
    return jnp.where(states == value, 1.0, 0.0).astype(BF)


def softmax_residual(diffs, states):
    top = jnp.maximum(jnp.maximum(diffs[0], diffs[1]), jnp.maximum(diffs[2], 0.0))
    exps = [jnp.exp(d - top) for d in diffs]
    inverse = 1.0 / (exps[0] + exps[1] + exps[2] + jnp.exp(-top))
    return [
        (jnp.where(states == a, 1.0, 0.0) - exps[a] * inverse).astype(BF) for a in range(3)
    ]


def exchange_kernel(
    left_in, right_in, lbias_in, rbias_in, coup_ref,
    grad_out, nat_out, rres_out, rhs_out, rg_out, lht_out,
    left_ref, right_ref, lbias_ref, rbias_ref, raw, flat, perm, spread, grads, nat, rres, rhs, lht, rt, loh, slt, bt,
    lp, xa, xb, zp, zb, rg,
    cs, cr, own, yp, yb, rr,
    in_sem, out_sem, lsend, lrecv, rsend, rrecv,
):
    row = lax.axis_index("row")
    col = lax.axis_index("col")
    core = lax.rem(row, 2)
    zl = lax.rem(lax.div(row, 2), 2)
    y = lax.div(row, 4)
    x = lax.div(col, 4)
    z = lax.rem(col, 4)

    def at_x(d):
        return {"row": row, "col": lax.rem(x + d, 4) * 4 + z}

    def at_z(d):
        return {"row": row, "col": x * 4 + lax.rem(z + d, 4)}

    def at_yz(d):
        return {"row": lax.rem(y + d // 2, 4) * 4 + lax.rem(zl + d % 2, 2) * 2 + core, "col": col}

    x_next, x_prev = at_x(1), at_x(3)
    core_peer = {"row": y * 4 + zl * 2 + 1 - core, "col": col}
    peers = (
        [at_x(d) for d in (1, 2, 3)] + [at_z(d) for d in (1, 2, 3)]
        + [at_yz(d) for d in range(1, 8)] + [core_peer]
    )

    barrier = pltpu.get_barrier_semaphore()
    for peer in peers:
        pl.semaphore_signal(barrier, inc=1, device_id=peer, device_id_type=MESH)

    loads = {}

    def load(key, src, dst):
        copy = pltpu.make_async_copy(src, dst, in_sem.at[len(loads)])
        copy.start()
        loads[key] = copy

    load("right", right_in, right_ref)
    for p in range(PIECES):
        rows = pl.ds(p * 1024, 1024)
        load(p, coup_ref.at[:, rows, :], raw.at[:, rows, :])
        if p == 0:
            load("left", left_in, left_ref)
            load("lbias", lbias_in, lbias_ref)
            load("rbias", rbias_in, rbias_ref)

    sent = []

    def send(src, dst, sems, slot, peer):
        copy = pltpu.make_async_remote_copy(
            src_ref=src, dst_ref=dst, send_sem=sems[0].at[slot], recv_sem=sems[1].at[slot],
            device_id=peer, device_id_type=MESH,
        )
        copy.start()
        sent.append(copy)
        return copy

    lsems = (lsend, lrecv)
    rsems = (rsend, rrecv)

    perm[...] = permutation(3)
    spread[...] = permutation(5)
    loads["right"].wait()
    right_t = right_ref[...].T
    for b in range(4):
        rt[pl.ds(b * 256, 256), :] = onehot(right_t, b)

    live = {}

    def left_fields(p):
        loads[p].wait()
        for a in range(4):
            for h in range(2):
                pair = [
                    raw[a, pl.ds(p * 1024 + (2 * h + k) * 256, 256), :] for k in range(2)
                ]
                turned = jnp.dot(
                    perm[...], jnp.concatenate(pair, axis=1), preferred_element_type=F32
                ).astype(BF)
                for k in range(2):
                    for jt in range(2):
                        for b in range(4):
                            flat[
                                pl.ds(a * 512 + p * 128 + (2 * h + k) * 32, 32),
                                pl.ds(b * 256 + jt * 128, 128),
                            ] = turned[(jt * 4 + b) * 32:(jt * 4 + b + 1) * 32, k * 128:(k + 1) * 128]
        lhs = jnp.concatenate([flat[pl.ds(a * 512 + p * 128, 128), :] for a in range(4)], axis=0)
        fields = jnp.dot(lhs, rt[...], preferred_element_type=F32)
        for a in range(3):
            diff = (fields[a * 128:(a + 1) * 128] - fields[384:512]).astype(BF)
            for xc in range(4):
                for zc in range(4):
                    lp[p, xc, zc, a] = diff[zc * 32:(zc + 1) * 32, xc * 128:(xc + 1) * 128]

    def x_scatter(p):
        if p in DIRECT_SCATTER:
            for d in (2, 1, 3):
                live[p, d] = send(lp.at[p, lax.rem(x + d, 4)], xb.at[p, d - 1], lsems, p * 16 + d, at_x(d))
            return
        opp, nxt, prv = lax.rem(x + 2, 4), lax.rem(x + 1, 4), lax.rem(x + 3, 4)
        lo, hi = pl.ds(0, 2), pl.ds(2, 2)
        live[p, 0] = send(lp.at[p, opp, lo], xa.at[p, 0], lsems, p * 16 + 0, x_next)
        live[p, 1] = send(lp.at[p, opp, hi], xa.at[p, 1], lsems, p * 16 + 1, x_prev)
        live[p, 2] = send(lp.at[p, nxt, hi], xb.at[p, 0, hi], lsems, p * 16 + 2, x_next)
        live[p, 3] = send(lp.at[p, prv, lo], xb.at[p, 1, lo], lsems, p * 16 + 3, x_prev)

    def x_relay(p):
        nxt, prv = lax.rem(x + 1, 4), lax.rem(x + 3, 4)
        lo, hi = pl.ds(0, 2), pl.ds(2, 2)
        live[p, 0].wait_recv()
        lp[p, nxt, lo] = (lp[p, nxt, lo].astype(F32) + xa[p, 0].astype(F32)).astype(BF)
        live[p, 4] = send(lp.at[p, nxt, lo], xb.at[p, 0, lo], lsems, p * 16 + 4, x_next)
        live[p, 1].wait_recv()
        lp[p, prv, hi] = (lp[p, prv, hi].astype(F32) + xa[p, 1].astype(F32)).astype(BF)
        live[p, 5] = send(lp.at[p, prv, hi], xb.at[p, 1, hi], lsems, p * 16 + 5, x_prev)

    def z_scatter(p):
        direct = p in DIRECT_SCATTER
        for m in (1, 2, 3) if direct else (2, 3, 4, 5):
            live[p, m].wait_recv()
        total = lp[p, x].astype(F32) + xb[p, 0].astype(F32) + xb[p, 1].astype(F32)
        if direct:
            total = total + xb[p, 2].astype(F32)
        zp[p] = total.astype(BF)
        for d in (2, 1, 3):
            live[p, 5 + d] = send(zp.at[p, lax.rem(z + d, 4)], zb.at[p, d - 1], lsems, p * 16 + 5 + d, at_z(d))

    def z_gather(p):
        for m in (6, 7, 8):
            live[p, m].wait_recv()
        total = zp[p, z].astype(F32)
        for k in range(3):
            total = total + zb[p, k].astype(F32)
        rows = pl.ds(pl.multiple_of(p * 128 + z * 32, 32), 32)
        diffs = [total[a] + bt[a, rows, :] for a in range(3)]
        result = softmax_residual(diffs, slt[x, rows, :])
        for a in range(3):
            rg[p, x, z, a] = result[a]
        block = rg.at[p, x, z]
        for d in (2, 1, 3):
            live[p, 8 + d] = send(block, block, lsems, p * 16 + 8 + d, at_z(d))

    def x_gather(p):
        for m in (9, 10, 11):
            live[p, m].wait_recv()
        block = rg.at[p, x]
        for d in (2, 1, 3) if p in DIRECT_GATHER else (1, 3):
            live[p, 11 + d] = send(block, block, lsems, p * 16 + 11 + d, at_x(d))

    def x_forward(p):
        nxt, prv = lax.rem(x + 1, 4), lax.rem(x + 3, 4)
        live[p, 12].wait_recv()
        block = rg.at[p, prv, pl.ds(0, 2)]
        live[p, 13] = send(block, block, lsems, p * 16 + 13, x_next)
        live[p, 14].wait_recv()
        block = rg.at[p, nxt, pl.ds(2, 2)]
        live[p, 15] = send(block, block, lsems, p * 16 + 15, x_prev)

    finals = []

    def keep(src, dst):
        copy = pltpu.make_async_copy(src, dst, out_sem.at[len(finals)])
        copy.start()
        finals.append(copy)

    def left_done(p):
        for m in (12, 13, 14) if p in DIRECT_GATHER else (13, 15):
            live[p, m].wait_recv()
        if p == PIECES - 1:
            keep(rg.at[p], rg_out)

    def gradient_piece(p):
        parts = piece_rows(rg[p])
        for a in range(4):
            turned = parts[a].astype(F32).T.astype(BF)
            nat[p * 4 + a] = turned
        keep(nat.at[pl.ds(p * 4, 4)], nat_out.at[pl.ds(p * 4, 4)])
        for h in range(2):
            lhs = jnp.concatenate(
                [
                    jnp.concatenate([parts[a], lht[a, pl.ds(p * 128, 128), :]], axis=1)
                    for a in (2 * h, 2 * h + 1)
                ],
                axis=0,
            )
            summed = jnp.dot(lhs, rhs[...], preferred_element_type=F32).astype(BF)
            for k in range(2):
                a = 2 * h + k

                def store(block, rows):
                    grads[a, pl.ds(p * 1024 + block * 256, 256), :] = rows

                spread_states(spread[...], summed[k * 128:(k + 1) * 128], store)
        rows = pl.ds(p * 1024, 1024)
        keep(grads.at[:, rows, :], grad_out.at[:, rows, :])

    def right_diffs(half):
        lhs = loh[pl.ds(pl.multiple_of(half * 256, 256), 256), :]
        fields = jnp.dot(lhs, flat[...], preferred_element_type=F32)
        return [fields[:, b * 256:(b + 1) * 256] - fields[:, 768:1024] for b in range(3)]

    def core_scatter():
        for b, diff in enumerate(right_diffs(1 - core)):
            cs[:, pl.ds(b * 256, 256)] = diff.astype(BF)
        live["c"] = send(cs, cr, rsems, 0, core_peer)

    def right_own():
        for b, diff in enumerate(right_diffs(core)):
            own[:, pl.ds(b * 256, 256)] = diff

    def yz_scatter():
        live["c"].wait_recv()
        for c in range(8):
            rows = pl.ds(c * 32, 32)
            yp[c] = (own[rows, :] + cr[rows, :].astype(F32)).astype(BF)
        for d in (5, 4, 3, 7, 2, 6, 1):
            chunk = lax.rem(y + d // 2, 4) * 2 + lax.rem(zl + d % 2, 2)
            live["s", d] = send(yp.at[chunk], yb.at[d - 1], rsems, d, at_yz(d))

    def right_rows(start, count):
        return pl.ds(pl.multiple_of(start, 32), count)

    def yz_gather():
        for d in range(1, 8):
            live["s", d].wait_recv()
        total = yp[y * 2 + zl].astype(F32)
        for k in range(7):
            total = total + yb[k].astype(F32)
        rows = right_rows(core * 256 + y * 64 + zl * 32, 32)
        base = rbias_ref[pl.ds(3, 1), :]
        diffs = [
            total[:, b * 256:(b + 1) * 256] + (rbias_ref[pl.ds(b, 1), :] - base) for b in range(3)
        ]
        for b, part in enumerate(softmax_residual(diffs, right_ref[rows, :])):
            rr[rows, pl.ds(b * 256, 256)] = part
        block = rr.at[rows, :]
        for d in (5, 4, 3, 7, 2, 6, 1):
            live["g", d] = send(block, block, rsems, 7 + d, at_yz(d))

    def core_gather():
        for d in range(1, 8):
            live["g", d].wait_recv()
        block = rr.at[right_rows(core * 256, 256), :]
        live["c1"] = send(block, block, rsems, 15, core_peer)

    def right_done():
        live["c1"].wait_recv()
        parts = four_states([rr[:, pl.ds(b * 256, 256)] for b in range(3)])
        for b in range(4):
            rhs[pl.ds(512, 512), pl.ds(b * 256, 256)] = -parts[b]
        keep(rhs, rhs_out)

    def right_spread():
        def store(block, rows):
            rres[pl.ds(block * 256, 256), :] = rows

        spread_states(spread[...], -rhs[pl.ds(512, 512), :], store)
        keep(rres, rres_out)

    def right_onehots():
        states = right_ref[...]
        for b in range(4):
            rhs[pl.ds(0, 512), pl.ds(b * 256, 256)] = -onehot(states, b)

    def left_tables():
        left_t = left_ref[...].T
        for xc in range(4):
            slt[xc] = left_t[:, xc * 128:(xc + 1) * 128]
        for a in range(4):
            lht[a] = onehot(left_t, a)
        keep(lht.at[:, pl.ds((PIECES - 1) * 128, 128), :], lht_out)
        base = lbias_ref[pl.ds(3, 1), :]
        for a in range(3):
            diff = lbias_ref[pl.ds(a, 1), :] - base
            for p in range(PIECES):
                part = jnp.broadcast_to(diff[:, p * 128:(p + 1) * 128], (128, 128))
                bt[a, pl.ds(p * 128, 128), :] = part.T

    def left_onehots():
        states = left_ref[...]
        for a in range(4):
            loh[:, pl.ds(a * 512, 512)] = onehot(states, a)

    left_fields(0)
    pl.semaphore_wait(barrier, len(peers))
    x_scatter(0)
    for p in (1, 2, 3):
        left_fields(p)
        x_scatter(p)
    for key in ("left", "lbias", "rbias"):
        loads[key].wait()
    left_onehots()
    core_scatter()
    z_scatter(0)
    right_own()
    x_relay(1)
    yz_scatter()
    x_relay(2)
    left_tables()
    right_onehots()
    z_gather(0)
    z_scatter(1)
    x_relay(3)
    z_scatter(2)
    x_gather(0)
    z_gather(1)
    z_scatter(3)
    yz_gather()
    z_gather(2)
    x_gather(1)
    z_gather(3)
    x_forward(0)
    x_gather(2)
    core_gather()
    x_gather(3)
    x_forward(1)
    right_done()
    left_done(0)
    x_forward(2)
    gradient_piece(0)
    right_spread()
    left_done(1)
    gradient_piece(1)
    left_done(2)
    gradient_piece(2)
    left_done(3)
    for copy in sent:
        copy.wait_send()
    for copy in finals:
        copy.wait()


def exchange(left_states, right_states, left_bias, right_bias, couplings):
    hbm = pl.BlockSpec(memory_space=pltpu.HBM)
    any_space = pl.BlockSpec(memory_space=pl.ANY)
    n = PIECES
    return pl.pallas_call(
        exchange_kernel,
        out_shape=(
            jax.ShapeDtypeStruct((4, 3072, 128), BF),
            jax.ShapeDtypeStruct((12, 512, 128), BF),
            jax.ShapeDtypeStruct((4096, 128), BF),
            jax.ShapeDtypeStruct((1024, 1024), BF),
            jax.ShapeDtypeStruct((4, 4, 3, 32, 128), BF),
            jax.ShapeDtypeStruct((4, 128, 512), BF),
        ),
        in_specs=[hbm] * 5,
        out_specs=(any_space,) * 6,
        scratch_shapes=[
            pltpu.VMEM((512, 512), jnp.int32),
            pltpu.VMEM((512, 256), jnp.int32),
            pltpu.VMEM((4, 512), F32),
            pltpu.VMEM((4, 256), F32),
            pltpu.VMEM((4, 4096, 128), BF),
            pltpu.VMEM((2048, 1024), BF),
            pltpu.VMEM((256, 256), BF),
            pltpu.VMEM((256, 256), BF),
            pltpu.VMEM((4, 3072, 128), BF),
            pltpu.VMEM((12, 512, 128), BF),
            pltpu.VMEM((4096, 128), BF),
            pltpu.VMEM((1024, 1024), BF),
            pltpu.VMEM((4, 512, 512), BF),
            pltpu.VMEM((1024, 512), BF),
            pltpu.VMEM((512, 2048), BF),
            pltpu.VMEM((4, 512, 128), jnp.int32),
            pltpu.VMEM((3, 512, 128), F32),
            pltpu.VMEM((n, 4, 4, 3, 32, 128), BF),
            pltpu.VMEM((n, 2, 2, 3, 32, 128), BF),
            pltpu.VMEM((n, 3, 4, 3, 32, 128), BF),
            pltpu.VMEM((n, 4, 3, 32, 128), BF),
            pltpu.VMEM((n, 3, 3, 32, 128), BF),
            pltpu.VMEM((n, 4, 4, 3, 32, 128), BF),
            pltpu.VMEM((256, 768), BF),
            pltpu.VMEM((256, 768), BF),
            pltpu.VMEM((256, 768), F32),
            pltpu.VMEM((8, 32, 768), BF),
            pltpu.VMEM((7, 32, 768), BF),
            pltpu.VMEM((512, 768), BF),
            pltpu.SemaphoreType.DMA((n + 4,)),
            pltpu.SemaphoreType.DMA((10,)),
            pltpu.SemaphoreType.DMA((n * 16,)),
            pltpu.SemaphoreType.DMA((n * 16,)),
            pltpu.SemaphoreType.DMA((16,)),
            pltpu.SemaphoreType.DMA((16,)),
        ],
        compiler_params=pltpu.CompilerParams(
            collective_id=0, has_side_effects=True, vmem_limit_bytes=EXCHANGE_VMEM
        ),
        name="exchange",
    )(*[pltpu.with_memory_space_constraint(v, pltpu.HBM) for v in (left_states, right_states, left_bias, right_bias, couplings)])


def finish_kernel(
    part_ref, nat_ref, rres_ref, rhs_ref, rg_ref, lht_ref,
    lres_out, rres_out, grad_out,
    grads, lres, sems,
):
    copies = []

    def put(src, dst):
        copy = pltpu.make_async_copy(src, dst, sems.at[len(copies)])
        copy.start()
        copies.append(copy)

    put(part_ref, grad_out.at[:, pl.ds(0, 3072), :])
    put(rres_ref, rres_out)
    spread = permutation(5)
    gather = permutation(4)
    parts = piece_rows(rg_ref[...])

    def last_piece(h):
        lhs = jnp.concatenate(
            [jnp.concatenate([parts[a], lht_ref[a]], axis=1) for a in (2 * h, 2 * h + 1)], axis=0
        )
        summed = jnp.dot(lhs, rhs_ref[...], preferred_element_type=F32).astype(BF)
        for k in range(2):
            a = 2 * h + k

            def store(block, rows):
                grads[a, pl.ds(block * 256, 256), :] = rows

            spread_states(spread, summed[k * 128:(k + 1) * 128], store)
        states = pl.ds(2 * h, 2)
        put(grads.at[states], grad_out.at[states, pl.ds(3072, 1024), :])

    last_piece(0)
    turned = [part.astype(F32).T.astype(BF) for part in parts]
    for q in range(4):
        for h in range(4 * q, 4 * q + 4):
            stack = side_by_side(
                [
                    [nat_ref[m, pl.ds((2 * h + k) * 16, 16), :] for m in range(12)]
                    + [block[(2 * h + k) * 16:(2 * h + k + 1) * 16] for block in turned]
                    for k in range(2)
                ]
            )
            rows = jnp.dot(gather, stack, preferred_element_type=F32).astype(BF)
            for k in range(2):
                lres[pl.ds((2 * h + k) * 256, 256), :] = rows[:, k * 128:(k + 1) * 128]
        block = pl.ds(q * 2048, 2048)
        put(lres.at[block, :], lres_out.at[block, :])
    last_piece(1)
    for copy in copies:
        copy.wait()


def finish(part, nat, rres, rhs, rg, lht):
    vmem = pl.BlockSpec(memory_space=pltpu.VMEM)
    any_space = pl.BlockSpec(memory_space=pl.ANY)
    return pl.pallas_call(
        finish_kernel,
        out_shape=(
            jax.ShapeDtypeStruct((8192, 128), BF),
            jax.ShapeDtypeStruct((4096, 128), BF),
            jax.ShapeDtypeStruct((4, 4096, 128), BF),
        ),
        in_specs=[any_space, vmem, any_space, vmem, vmem, vmem],
        out_specs=(pl.BlockSpec(memory_space=pltpu.HBM),) * 3,
        scratch_shapes=[
            pltpu.VMEM((4, 1024, 128), BF),
            pltpu.VMEM((8192, 128), BF),
            pltpu.SemaphoreType.DMA((8,)),
        ],
        compiler_params=pltpu.CompilerParams(vmem_limit_bytes=FINISH_VMEM),
        name="finish",
    )(part, nat, rres, rhs, rg, lht)


def body(left_states, right_states, left_bias, right_bias, couplings):
    view = couplings.reshape(4, 512, 4, 2, 128).transpose(0, 1, 3, 2, 4).reshape(4, 4096, 128)
    kept = exchange(left_states, right_states, left_bias, right_bias, view)
    left, right, grad = finish(*kept)
    left_residual = left.reshape(512, 4, 4, 128).transpose(0, 2, 1, 3).reshape(512, 4, 512)
    right_residual = right.reshape(512, 2, 4, 128).transpose(0, 2, 1, 3).reshape(512, 4, 256)
    coupling_grad = grad.reshape(4, 512, 2, 4, 128).transpose(0, 1, 3, 2, 4).reshape(4, 512, 4, 256)
    return left_residual, right_residual, coupling_grad


def solution(mesh):
    in_specs = (
        P(None, "row"),
        P(None, "col"),
        P(None, "row"),
        P(None, "col"),
        P(None, "row", None, "col"),
    )
    out_specs = (P(None, None, "row"), P(None, None, "col"), P(None, "row", None, "col"))
    return jax.shard_map(body, mesh=mesh, in_specs=in_specs, out_specs=out_specs, check_vma=False)
```

time: 380 us -> 60.7 us (0.16)
  the two profiles are of different devices: /device:TPU:16 before, /device:TPU:6 now
where the time goes in v2:
time: 60.7 us; the launch traced here: 60.6 us
  Pallas kernels  59.8 us (99%)
  between operations  0.8 us (1%)
    pallas_call x1, Pallas kernels, exchange(): pl.pallas_call(exchange_kernel, out_shape=(jax.ShapeDtypeStruct((4, 3072,...  56.6 us
    pallas_call x1, Pallas kernels, finish(): pl.pallas_call(finish_kernel, out_shape=(jax.ShapeDtypeStruct((8192, 128)...  3.19 us

profile of v2, /device:TPU:6, one launch (start us, length us, event | category | flops | bytes accessed | tf_op | source)
XLA Modules:
  0.0 60.6 jit_solution(14116546874810749704)
XLA Ops:
  0.6 56.6 %exchange.1 = (bf16[4,3072,128]{2,1,0:T(8,128)(2,1)S(1)}, bf16[12,512,128]{2,1,0:T(8,128)(2,1)S(1)}, bf16[4096,128]{1,0:T(8,128)(2,1)S(1)}, bf16[1024,1024]{1,0:...) custom-call(s32[512,512]{1,0:T(8,128)} %left_in.1, s32[512,256]{1,0:T(8,128)} %right_in.1, ...), custom_call_target="tpu_custom_call" | custom-call | tf_op jit(solution)/shard_map/exchange/pallas_call | solution.py:415
  57.3 3.2 %finish.1 = (bf16[8192,128]{1,0:T(8,128)(2,1)}, bf16[4096,128]{1,0:T(8,128)(2,1)}, bf16[4,4096,128]{2,1,0:T(8,128)(2,1)}) custom-call(bf16[4,3072,128]{2,1,0:T(8,128)(2,1)S(1)} %get-tuple-element.12.part_ref, bf16[12,512,128]{2,1,0:T(8,128)(2,1)S(1)} %get-tuple-element.13.nat_ref, bf16[4096,128]{1,0:T(8,128)(2,1)S(1)} %get-tuple-element.14.rres_ref, ...), custom_call_target="tpu_custom_call" | custom-call | tf_op jit(solution)/shard_map/finish/pallas_call | solution.py:528

commit v3 on v2

--- a/solution.py
+++ b/solution.py
@@ -11,6 +11,7 @@
 PIECES = 4
 DIRECT_SCATTER = (0,)
 DIRECT_GATHER = (3,)
+Z_FIRST = (1,)
 EXCHANGE_VMEM = 40 * 1024 * 1024
 FINISH_VMEM = 24 * 1024 * 1024
 
@@ -75,7 +76,7 @@
     grad_out, nat_out, rres_out, rhs_out, rg_out, lht_out,
     left_ref, right_ref, lbias_ref, rbias_ref, raw, flat, perm, spread, grads, nat, rres, rhs, lht, rt, loh, slt, bt,
     lp, xa, xb, zp, zb, rg,
-    cs, cr, own, yp, yb, rr,
+    cs, cr, own, yp, yb, tz, zs, zr, rr,
     in_sem, out_sem, lsend, lrecv, rsend, rrecv,
 ):
     row = lax.axis_index("row")
@@ -92,15 +93,20 @@
     def at_z(d):
         return {"row": row, "col": x * 4 + lax.rem(z + d, 4)}
 
-    def at_yz(d):
-        return {"row": lax.rem(y + d // 2, 4) * 4 + lax.rem(zl + d % 2, 2) * 2 + core, "col": col}
-
-    x_next, x_prev = at_x(1), at_x(3)
+    def at_y(d):
+        return {"row": lax.rem(y + d, 4) * 4 + zl * 2 + core, "col": col}
+
     core_peer = {"row": y * 4 + zl * 2 + 1 - core, "col": col}
-    peers = (
-        [at_x(d) for d in (1, 2, 3)] + [at_z(d) for d in (1, 2, 3)]
-        + [at_yz(d) for d in range(1, 8)] + [core_peer]
-    )
+    zl_peer = {"row": y * 4 + (1 - zl) * 2 + core, "col": col}
+    peers = [at(d) for at in (at_x, at_z, at_y) for d in (1, 2, 3)] + [zl_peer, core_peer]
+
+    def axes(p):
+        return ((z, at_z), (x, at_x)) if p in Z_FIRST else ((x, at_x), (z, at_z))
+
+    def chunk(ref, p, index, part=pl.ds(0, 4)):
+        return ref.at[p, part, index] if p in Z_FIRST else ref.at[p, index, part]
+
+    low, high = pl.ds(0, 2), pl.ds(2, 2)
 
     barrier = pltpu.get_barrier_semaphore()
     for peer in peers:
@@ -170,43 +176,46 @@
                 for zc in range(4):
                     lp[p, xc, zc, a] = diff[zc * 32:(zc + 1) * 32, xc * 128:(xc + 1) * 128]
 
-    def x_scatter(p):
+    def first_scatter(p):
+        me, at = axes(p)[0]
         if p in DIRECT_SCATTER:
             for d in (2, 1, 3):
-                live[p, d] = send(lp.at[p, lax.rem(x + d, 4)], xb.at[p, d - 1], lsems, p * 16 + d, at_x(d))
+                live[p, d] = send(chunk(lp, p, lax.rem(me + d, 4)), xb.at[p, d - 1], lsems, p * 16 + d, at(d))
             return
-        opp, nxt, prv = lax.rem(x + 2, 4), lax.rem(x + 1, 4), lax.rem(x + 3, 4)
-        lo, hi = pl.ds(0, 2), pl.ds(2, 2)
-        live[p, 0] = send(lp.at[p, opp, lo], xa.at[p, 0], lsems, p * 16 + 0, x_next)
-        live[p, 1] = send(lp.at[p, opp, hi], xa.at[p, 1], lsems, p * 16 + 1, x_prev)
-        live[p, 2] = send(lp.at[p, nxt, hi], xb.at[p, 0, hi], lsems, p * 16 + 2, x_next)
-        live[p, 3] = send(lp.at[p, prv, lo], xb.at[p, 1, lo], lsems, p * 16 + 3, x_prev)
-
-    def x_relay(p):
-        nxt, prv = lax.rem(x + 1, 4), lax.rem(x + 3, 4)
-        lo, hi = pl.ds(0, 2), pl.ds(2, 2)
+        opp, nxt, prv = lax.rem(me + 2, 4), lax.rem(me + 1, 4), lax.rem(me + 3, 4)
+        live[p, 0] = send(chunk(lp, p, opp, low), xa.at[p, 0], lsems, p * 16 + 0, at(1))
+        live[p, 1] = send(chunk(lp, p, opp, high), xa.at[p, 1], lsems, p * 16 + 1, at(3))
+        live[p, 2] = send(chunk(lp, p, nxt, high), xb.at[p, 0, high], lsems, p * 16 + 2, at(1))
+        live[p, 3] = send(chunk(lp, p, prv, low), xb.at[p, 1, low], lsems, p * 16 + 3, at(3))
+
+    def relay(p):
+        me, at = axes(p)[0]
+        mine = chunk(lp, p, lax.rem(me + 1, 4), low)
         live[p, 0].wait_recv()
-        lp[p, nxt, lo] = (lp[p, nxt, lo].astype(F32) + xa[p, 0].astype(F32)).astype(BF)
-        live[p, 4] = send(lp.at[p, nxt, lo], xb.at[p, 0, lo], lsems, p * 16 + 4, x_next)
+        mine[...] = (mine[...].astype(F32) + xa[p, 0].astype(F32)).astype(BF)
+        live[p, 4] = send(mine, xb.at[p, 0, low], lsems, p * 16 + 4, at(1))
+        mine = chunk(lp, p, lax.rem(me + 3, 4), high)
         live[p, 1].wait_recv()
-        lp[p, prv, hi] = (lp[p, prv, hi].astype(F32) + xa[p, 1].astype(F32)).astype(BF)
-        live[p, 5] = send(lp.at[p, prv, hi], xb.at[p, 1, hi], lsems, p * 16 + 5, x_prev)
-
-    def z_scatter(p):
+        mine[...] = (mine[...].astype(F32) + xa[p, 1].astype(F32)).astype(BF)
+        live[p, 5] = send(mine, xb.at[p, 1, high], lsems, p * 16 + 5, at(3))
+
+    def second_scatter(p):
+        (first, _), (me, at) = axes(p)
         direct = p in DIRECT_SCATTER
         for m in (1, 2, 3) if direct else (2, 3, 4, 5):
             live[p, m].wait_recv()
-        total = lp[p, x].astype(F32) + xb[p, 0].astype(F32) + xb[p, 1].astype(F32)
+        total = chunk(lp, p, first)[...].astype(F32) + xb[p, 0].astype(F32) + xb[p, 1].astype(F32)
         if direct:
             total = total + xb[p, 2].astype(F32)
         zp[p] = total.astype(BF)
         for d in (2, 1, 3):
-            live[p, 5 + d] = send(zp.at[p, lax.rem(z + d, 4)], zb.at[p, d - 1], lsems, p * 16 + 5 + d, at_z(d))
-
-    def z_gather(p):
+            live[p, 5 + d] = send(zp.at[p, lax.rem(me + d, 4)], zb.at[p, d - 1], lsems, p * 16 + 5 + d, at(d))
+
+    def first_gather(p):
+        me, at = axes(p)[1]
         for m in (6, 7, 8):
             live[p, m].wait_recv()
-        total = zp[p, z].astype(F32)
+        total = zp[p, me].astype(F32)
         for k in range(3):
             total = total + zb[p, k].astype(F32)
         rows = pl.ds(pl.multiple_of(p * 128 + z * 32, 32), 32)
@@ -216,23 +225,24 @@
             rg[p, x, z, a] = result[a]
         block = rg.at[p, x, z]
         for d in (2, 1, 3):
-            live[p, 8 + d] = send(block, block, lsems, p * 16 + 8 + d, at_z(d))
-
-    def x_gather(p):
+            live[p, 8 + d] = send(block, block, lsems, p * 16 + 8 + d, at(d))
+
+    def second_gather(p):
+        me, at = axes(p)[0]
         for m in (9, 10, 11):
             live[p, m].wait_recv()
-        block = rg.at[p, x]
+        block = chunk(rg, p, me)
         for d in (2, 1, 3) if p in DIRECT_GATHER else (1, 3):
-            live[p, 11 + d] = send(block, block, lsems, p * 16 + 11 + d, at_x(d))
-
-    def x_forward(p):
-        nxt, prv = lax.rem(x + 1, 4), lax.rem(x + 3, 4)
+            live[p, 11 + d] = send(block, block, lsems, p * 16 + 11 + d, at(d))
+
+    def forward(p):
+        me, at = axes(p)[0]
         live[p, 12].wait_recv()
-        block = rg.at[p, prv, pl.ds(0, 2)]
-        live[p, 13] = send(block, block, lsems, p * 16 + 13, x_next)
+        block = chunk(rg, p, lax.rem(me + 3, 4), low)
+        live[p, 13] = send(block, block, lsems, p * 16 + 13, at(1))
         live[p, 14].wait_recv()
-        block = rg.at[p, nxt, pl.ds(2, 2)]
-        live[p, 15] = send(block, block, lsems, p * 16 + 15, x_prev)
+        block = chunk(rg, p, lax.rem(me + 1, 4), high)
+        live[p, 15] = send(block, block, lsems, p * 16 + 15, at(3))
 
     finals = []
 
@@ -286,24 +296,31 @@
         for b, diff in enumerate(right_diffs(core)):
             own[:, pl.ds(b * 256, 256)] = diff
 
-    def yz_scatter():
+    def y_scatter():
         live["c"].wait_recv()
-        for c in range(8):
-            rows = pl.ds(c * 32, 32)
+        for c in range(4):
+            rows = pl.ds(c * 64, 64)
             yp[c] = (own[rows, :] + cr[rows, :].astype(F32)).astype(BF)
-        for d in (5, 4, 3, 7, 2, 6, 1):
-            chunk = lax.rem(y + d // 2, 4) * 2 + lax.rem(zl + d % 2, 2)
-            live["s", d] = send(yp.at[chunk], yb.at[d - 1], rsems, d, at_yz(d))
+        for d in (2, 1, 3):
+            live["ys", d] = send(yp.at[lax.rem(y + d, 4)], yb.at[d - 1], rsems, d, at_y(d))
+
+    def zl_scatter():
+        for d in (1, 2, 3):
+            live["ys", d].wait_recv()
+        total = yp[y].astype(F32)
+        for k in range(3):
+            total = total + yb[k].astype(F32)
+        tz[0] = total[:32]
+        tz[1] = total[32:]
+        zs[...] = tz[1 - zl].astype(BF)
+        live["zs"] = send(zs, zr, rsems, 4, zl_peer)
 
     def right_rows(start, count):
         return pl.ds(pl.multiple_of(start, 32), count)
 
-    def yz_gather():
-        for d in range(1, 8):
-            live["s", d].wait_recv()
-        total = yp[y * 2 + zl].astype(F32)
-        for k in range(7):
-            total = total + yb[k].astype(F32)
+    def zl_gather():
+        live["zs"].wait_recv()
+        total = tz[zl] + zr[...].astype(F32)
         rows = right_rows(core * 256 + y * 64 + zl * 32, 32)
         base = rbias_ref[pl.ds(3, 1), :]
         diffs = [
@@ -312,14 +329,19 @@
         for b, part in enumerate(softmax_residual(diffs, right_ref[rows, :])):
             rr[rows, pl.ds(b * 256, 256)] = part
         block = rr.at[rows, :]
-        for d in (5, 4, 3, 7, 2, 6, 1):
-            live["g", d] = send(block, block, rsems, 7 + d, at_yz(d))
+        live["zg"] = send(block, block, rsems, 5, zl_peer)
+
+    def y_gather():
+        live["zg"].wait_recv()
+        block = rr.at[right_rows(core * 256 + y * 64, 64), :]
+        for d in (2, 1, 3):
+            live["yg", d] = send(block, block, rsems, 5 + d, at_y(d))
 
     def core_gather():
-        for d in range(1, 8):
-            live["g", d].wait_recv()
+        for d in (1, 2, 3):
+            live["yg", d].wait_recv()
         block = rr.at[right_rows(core * 256, 256), :]
-        live["c1"] = send(block, block, rsems, 15, core_peer)
+        live["c1"] = send(block, block, rsems, 9, core_peer)
 
     def right_done():
         live["c1"].wait_recv()
@@ -360,47 +382,52 @@
             loh[:, pl.ds(a * 512, 512)] = onehot(states, a)
 
     left_fields(0)
-    pl.semaphore_wait(barrier, len(peers))
-    x_scatter(0)
-    for p in (1, 2, 3):
-        left_fields(p)
-        x_scatter(p)
     for key in ("left", "lbias", "rbias"):
         loads[key].wait()
     left_onehots()
+    pl.semaphore_wait(barrier, len(peers))
+    first_scatter(0)
+    left_fields(1)
+    left_fields(2)
+    first_scatter(1)
+    first_scatter(2)
+    left_fields(3)
     core_scatter()
-    z_scatter(0)
     right_own()
-    x_relay(1)
-    yz_scatter()
-    x_relay(2)
     left_tables()
+    second_scatter(0)
+    relay(2)
+    relay(1)
+    y_scatter()
+    first_scatter(3)
+    second_scatter(2)
+    first_gather(0)
+    second_scatter(1)
+    relay(3)
+    zl_scatter()
+    first_gather(2)
+    first_gather(1)
+    second_gather(0)
+    zl_gather()
     right_onehots()
-    z_gather(0)
-    z_scatter(1)
-    x_relay(3)
-    z_scatter(2)
-    x_gather(0)
-    z_gather(1)
-    z_scatter(3)
-    yz_gather()
-    z_gather(2)
-    x_gather(1)
-    z_gather(3)
-    x_forward(0)
-    x_gather(2)
+    second_scatter(3)
+    second_gather(1)
+    y_gather()
+    second_gather(2)
+    forward(0)
+    first_gather(3)
+    forward(2)
+    forward(1)
     core_gather()
-    x_gather(3)
-    x_forward(1)
+    second_gather(3)
+    left_done(0)
+    left_done(2)
     right_done()
-    left_done(0)
-    x_forward(2)
     gradient_piece(0)
     right_spread()
     left_done(1)
+    gradient_piece(2)
     gradient_piece(1)
-    left_done(2)
-    gradient_piece(2)
     left_done(3)
     for copy in sent:
         copy.wait_send()
@@ -451,15 +478,18 @@
             pltpu.VMEM((256, 768), BF),
             pltpu.VMEM((256, 768), BF),
             pltpu.VMEM((256, 768), F32),
-            pltpu.VMEM((8, 32, 768), BF),
-            pltpu.VMEM((7, 32, 768), BF),
+            pltpu.VMEM((4, 64, 768), BF),
+            pltpu.VMEM((3, 64, 768), BF),
+            pltpu.VMEM((2, 32, 768), F32),
+            pltpu.VMEM((32, 768), BF),
+            pltpu.VMEM((32, 768), BF),
             pltpu.VMEM((512, 768), BF),
             pltpu.SemaphoreType.DMA((n + 4,)),
             pltpu.SemaphoreType.DMA((10,)),
             pltpu.SemaphoreType.DMA((n * 16,)),
             pltpu.SemaphoreType.DMA((n * 16,)),
-            pltpu.SemaphoreType.DMA((16,)),
-            pltpu.SemaphoreType.DMA((16,)),
+            pltpu.SemaphoreType.DMA((10,)),
+            pltpu.SemaphoreType.DMA((10,)),
         ],
         compiler_params=pltpu.CompilerParams(
             collective_id=0, has_side_effects=True, vmem_limit_bytes=EXCHANGE_VMEM

time: 60.7 us -> 55.1 us (0.908)
  the two profiles are of different devices: /device:TPU:6 before, /device:TPU:1 now
where the time goes in v3:
time: 55.1 us; the launch traced here: 55 us
  Pallas kernels  54.2 us (98%)
  between operations  0.8 us (1%)
    pallas_call x1, Pallas kernels, exchange(): pl.pallas_call(exchange_kernel, out_shape=(jax.ShapeDtypeStruct((4, 3072,...  51 us
    pallas_call x1, Pallas kernels, finish(): pl.pallas_call(finish_kernel, out_shape=(jax.ShapeDtypeStruct((8192, 128)...  3.19 us

profile of v3, /device:TPU:1, one launch (start us, length us, event | category | flops | bytes accessed | tf_op | source)
XLA Modules:
  0.0 55.0 jit_solution(3982704098125681897)
XLA Ops:
  0.6 51.0 %exchange.1 = (bf16[4,3072,128]{2,1,0:T(8,128)(2,1)S(1)}, bf16[12,512,128]{2,1,0:T(8,128)(2,1)S(1)}, bf16[4096,128]{1,0:T(8,128)(2,1)S(1)}, bf16[1024,1024]{1,0:...) custom-call(s32[512,512]{1,0:T(8,128)} %left_in.1, s32[512,256]{1,0:T(8,128)} %right_in.1, ...), custom_call_target="tpu_custom_call" | custom-call | tf_op jit(solution)/shard_map/exchange/pallas_call | solution.py:442
  51.7 3.2 %finish.1 = (bf16[8192,128]{1,0:T(8,128)(2,1)}, bf16[4096,128]{1,0:T(8,128)(2,1)}, bf16[4,4096,128]{2,1,0:T(8,128)(2,1)}) custom-call(bf16[4,3072,128]{2,1,0:T(8,128)(2,1)S(1)} %get-tuple-element.12.part_ref, bf16[12,512,128]{2,1,0:T(8,128)(2,1)S(1)} %get-tuple-element.13.nat_ref, bf16[4096,128]{1,0:T(8,128)(2,1)S(1)} %get-tuple-element.14.rres_ref, ...), custom_call_target="tpu_custom_call" | custom-call | tf_op jit(solution)/shard_map/finish/pallas_call | solution.py:558

commit v4 on v3

--- a/solution.py
+++ b/solution.py
@@ -10,7 +10,7 @@
 F32 = jnp.float32
 PIECES = 4
 DIRECT_SCATTER = (0,)
-DIRECT_GATHER = (3,)
+DIRECT_GATHER = (0, 3)
 Z_FIRST = (1,)
 EXCHANGE_VMEM = 40 * 1024 * 1024
 FINISH_VMEM = 24 * 1024 * 1024
@@ -62,6 +62,24 @@
     return jnp.where(states == value, 1.0, 0.0).astype(BF)
 
 
+def piece_gradient(parts, heads, rhs, right_sum):
+    lhs = jnp.concatenate(
+        [jnp.concatenate([parts[a], heads[a]], axis=1) for a in range(3)], axis=0
+    )
+    nine = jnp.dot(lhs, rhs[:, pl.ds(0, 768)], preferred_element_type=F32)
+    sums = [jnp.sum(parts[a].astype(F32), axis=1, keepdims=True) for a in range(3)]
+    blocks = []
+    for a in range(3):
+        row = [nine[a * 128:(a + 1) * 128, b * 256:(b + 1) * 256] for b in range(3)]
+        blocks.append(row + [-sums[a] - (row[0] + row[1] + row[2])])
+    last = [
+        right_sum[pl.ds(0, 1), pl.ds(b * 256, 256)] - (blocks[0][b] + blocks[1][b] + blocks[2][b])
+        for b in range(3)
+    ]
+    blocks.append(last + [(sums[0] + sums[1] + sums[2]) - (last[0] + last[1] + last[2])])
+    return [jnp.concatenate([block.astype(BF) for block in row], axis=1) for row in blocks]
+
+
 def softmax_residual(diffs, states):
     top = jnp.maximum(jnp.maximum(diffs[0], diffs[1]), jnp.maximum(diffs[2], 0.0))
     exps = [jnp.exp(d - top) for d in diffs]
@@ -74,7 +92,7 @@
 def exchange_kernel(
     left_in, right_in, lbias_in, rbias_in, coup_ref,
     grad_out, nat_out, rres_out, rhs_out, rg_out, lht_out,
-    left_ref, right_ref, lbias_ref, rbias_ref, raw, flat, perm, spread, grads, nat, rres, rhs, lht, rt, loh, slt, bt,
+    left_ref, right_ref, lbias_ref, rbias_ref, raw, flat, perm, spread, grads, nat, rres, rhs, rsum, lht, rt, loh, slt, bt,
     lp, xa, xb, zp, zb, rg,
     cs, cr, own, yp, yb, tz, zs, zr, rr,
     in_sem, out_sem, lsend, lrecv, rsend, rrecv,
@@ -263,22 +281,13 @@
             turned = parts[a].astype(F32).T.astype(BF)
             nat[p * 4 + a] = turned
         keep(nat.at[pl.ds(p * 4, 4)], nat_out.at[pl.ds(p * 4, 4)])
-        for h in range(2):
-            lhs = jnp.concatenate(
-                [
-                    jnp.concatenate([parts[a], lht[a, pl.ds(p * 128, 128), :]], axis=1)
-                    for a in (2 * h, 2 * h + 1)
-                ],
-                axis=0,
-            )
-            summed = jnp.dot(lhs, rhs[...], preferred_element_type=F32).astype(BF)
-            for k in range(2):
-                a = 2 * h + k
-
-                def store(block, rows):
-                    grads[a, pl.ds(p * 1024 + block * 256, 256), :] = rows
-
-                spread_states(spread[...], summed[k * 128:(k + 1) * 128], store)
+        heads = [lht[a, pl.ds(p * 128, 128), :] for a in range(3)]
+        for a, values in enumerate(piece_gradient(parts, heads, rhs, rsum)):
+
+            def store(block, rows):
+                grads[a, pl.ds(p * 1024 + block * 256, 256), :] = rows
+
+            spread_states(spread[...], values, store)
         rows = pl.ds(p * 1024, 1024)
         keep(grads.at[:, rows, :], grad_out.at[:, rows, :])
 
@@ -348,6 +357,9 @@
         parts = four_states([rr[:, pl.ds(b * 256, 256)] for b in range(3)])
         for b in range(4):
             rhs[pl.ds(512, 512), pl.ds(b * 256, 256)] = -parts[b]
+        for b in range(3):
+            total = jnp.sum(-parts[b].astype(F32), axis=0, keepdims=True)
+            rsum[:, pl.ds(b * 256, 256)] = jnp.broadcast_to(total, (8, 256))
         keep(rhs, rhs_out)
 
     def right_spread():
@@ -382,52 +394,51 @@
             loh[:, pl.ds(a * 512, 512)] = onehot(states, a)
 
     left_fields(0)
+    pl.semaphore_wait(barrier, len(peers))
+    first_scatter(0)
+    left_fields(1)
+    first_scatter(1)
+    left_fields(2)
+    left_fields(3)
+    first_scatter(2)
     for key in ("left", "lbias", "rbias"):
         loads[key].wait()
     left_onehots()
-    pl.semaphore_wait(barrier, len(peers))
-    first_scatter(0)
-    left_fields(1)
-    left_fields(2)
-    first_scatter(1)
-    first_scatter(2)
-    left_fields(3)
     core_scatter()
+    first_scatter(3)
+    second_scatter(0)
     right_own()
+    relay(2)
+    y_scatter()
+    right_onehots()
+    relay(1)
+    second_scatter(2)
     left_tables()
-    second_scatter(0)
-    relay(2)
-    relay(1)
-    y_scatter()
-    first_scatter(3)
-    second_scatter(2)
     first_gather(0)
+    relay(3)
     second_scatter(1)
-    relay(3)
     zl_scatter()
     first_gather(2)
     first_gather(1)
+    zl_gather()
     second_gather(0)
-    zl_gather()
-    right_onehots()
     second_scatter(3)
     second_gather(1)
+    second_gather(2)
     y_gather()
-    second_gather(2)
-    forward(0)
     first_gather(3)
     forward(2)
+    core_gather()
     forward(1)
-    core_gather()
     second_gather(3)
     left_done(0)
     left_done(2)
     right_done()
+    right_spread()
+    gradient_piece(2)
+    left_done(1)
+    gradient_piece(1)
     gradient_piece(0)
-    right_spread()
-    left_done(1)
-    gradient_piece(2)
-    gradient_piece(1)
     left_done(3)
     for copy in sent:
         copy.wait_send()
@@ -464,6 +475,7 @@
             pltpu.VMEM((12, 512, 128), BF),
             pltpu.VMEM((4096, 128), BF),
             pltpu.VMEM((1024, 1024), BF),
+            pltpu.VMEM((8, 768), F32),
             pltpu.VMEM((4, 512, 512), BF),
             pltpu.VMEM((1024, 512), BF),
             pltpu.VMEM((512, 2048), BF),

time: 55.1 us -> 55.3 us (level)
  the two profiles are of different devices: /device:TPU:1 before, /device:TPU:16 now
where the time goes in v4:
time: 55.3 us; the launch traced here: 55.2 us
  Pallas kernels  54.4 us (98%)
  between operations  0.8 us (1%)
    pallas_call x1, Pallas kernels, exchange(): pl.pallas_call(exchange_kernel, out_shape=(jax.ShapeDtypeStruct((4, 3072,...  51.2 us
    pallas_call x1, Pallas kernels, finish(): pl.pallas_call(finish_kernel, out_shape=(jax.ShapeDtypeStruct((8192, 128)...  3.19 us

profile of v4, /device:TPU:16, one launch (start us, length us, event | category | flops | bytes accessed | tf_op | source)
XLA Modules:
  0.0 55.2 jit_solution(12773000536363156116)
XLA Ops:
  0.6 51.2 %exchange.1 = (bf16[4,3072,128]{2,1,0:T(8,128)(2,1)S(1)}, bf16[12,512,128]{2,1,0:T(8,128)(2,1)S(1)}, bf16[4096,128]{1,0:T(8,128)(2,1)S(1)}, bf16[1024,1024]{1,0:...) custom-call(s32[512,512]{1,0:T(8,128)} %left_in.1, s32[512,256]{1,0:T(8,128)} %right_in.1, ...), custom_call_target="tpu_custom_call" | custom-call | tf_op jit(solution)/shard_map/exchange/pallas_call | solution.py:453
  51.9 3.2 %finish.1 = (bf16[8192,128]{1,0:T(8,128)(2,1)}, bf16[4096,128]{1,0:T(8,128)(2,1)}, bf16[4,4096,128]{2,1,0:T(8,128)(2,1)}) custom-call(bf16[4,3072,128]{2,1,0:T(8,128)(2,1)S(1)} %get-tuple-element.12.part_ref, bf16[12,512,128]{2,1,0:T(8,128)(2,1)S(1)} %get-tuple-element.13.nat_ref, bf16[4096,128]{1,0:T(8,128)(2,1)S(1)} %get-tuple-element.14.rres_ref, ...), custom_call_target="tpu_custom_call" | custom-call | tf_op jit(solution)/shard_map/finish/pallas_call | solution.py:570

commit v5 on v4

--- a/solution.py
+++ b/solution.py
@@ -399,8 +399,8 @@
     left_fields(1)
     first_scatter(1)
     left_fields(2)
+    first_scatter(2)
     left_fields(3)
-    first_scatter(2)
     for key in ("left", "lbias", "rbias"):
         loads[key].wait()
     left_onehots()
@@ -410,7 +410,6 @@
     right_own()
     relay(2)
     y_scatter()
-    right_onehots()
     relay(1)
     second_scatter(2)
     left_tables()
@@ -426,6 +425,7 @@
     second_gather(1)
     second_gather(2)
     y_gather()
+    right_onehots()
     first_gather(3)
     forward(2)
     core_gather()
@@ -434,8 +434,8 @@
     left_done(0)
     left_done(2)
     right_done()
+    gradient_piece(2)
     right_spread()
-    gradient_piece(2)
     left_done(1)
     gradient_piece(1)
     gradient_piece(0)

time: 55.3 us -> 54.9 us (level); the launches traced: 55.2 us -> 53.9 us
  Pallas kernels: 54.4 us -> 53.1 us
    pallas_call x1, Pallas kernels: 51.2 us -> 49.9 us  [exchange(): pl.pallas_call(exchange_kernel, out_shape=(jax.ShapeDtypeStruct((4, 3072,...]
where the time goes in v5:
time: 54.9 us; the launch traced here: 53.9 us
  Pallas kernels  53.1 us (97%)
  between operations  0.8 us (1%)
    pallas_call x1, Pallas kernels, exchange(): pl.pallas_call(exchange_kernel, out_shape=(jax.ShapeDtypeStruct((4, 3072,...  49.9 us
    pallas_call x1, Pallas kernels, finish(): pl.pallas_call(finish_kernel, out_shape=(jax.ShapeDtypeStruct((8192, 128)...  3.19 us

profile of v5, /device:TPU:16, one launch (start us, length us, event | category | flops | bytes accessed | tf_op | source)
XLA Modules:
  0.0 53.9 jit_solution(8367763924751661240)
XLA Ops:
  0.6 49.9 %exchange.1 = (bf16[4,3072,128]{2,1,0:T(8,128)(2,1)S(1)}, bf16[12,512,128]{2,1,0:T(8,128)(2,1)S(1)}, bf16[4096,128]{1,0:T(8,128)(2,1)S(1)}, bf16[1024,1024]{1,0:...) custom-call(s32[512,512]{1,0:T(8,128)} %left_in.1, s32[512,256]{1,0:T(8,128)} %right_in.1, ...), custom_call_target="tpu_custom_call" | custom-call | tf_op jit(solution)/shard_map/exchange/pallas_call | solution.py:453
  50.5 3.2 %finish.1 = (bf16[8192,128]{1,0:T(8,128)(2,1)}, bf16[4096,128]{1,0:T(8,128)(2,1)}, bf16[4,4096,128]{2,1,0:T(8,128)(2,1)}) custom-call(bf16[4,3072,128]{2,1,0:T(8,128)(2,1)S(1)} %get-tuple-element.12.part_ref, bf16[12,512,128]{2,1,0:T(8,128)(2,1)S(1)} %get-tuple-element.13.nat_ref, bf16[4096,128]{1,0:T(8,128)(2,1)S(1)} %get-tuple-element.14.rres_ref, ...), custom_call_target="tpu_custom_call" | custom-call | tf_op jit(solution)/shard_map/finish/pallas_call | solution.py:570
